TPU v7x, 32 devices: a whole 2x2x4 slice. The times are simulated.
32 devices in a mesh: lst: 4 (over y, x), night: 8 (over z, core).
Axes of the slice: x: 2, y: 2, z: 4, core: 2. Of those that a mesh axis runs over, the one named last changes fastest.
Arguments:
- visibility: bfloat16 [8, 32, 16, 2, 1536], P('night', 'lst'), may hold values from -18 to 18
- flags: int32 [8, 32, 16, 1536], P('night', 'lst'), may hold values 0 or 1
- counts: int32 [8, 32], P('night', 'lst'), may hold values from 1 to 4
- offsets: int32 [8], P('night'), may hold values from -6 to 6, as said below
- fraction: float32 [8], P('night'), may hold values from 0 to 1
- gains: float32 [8, 2, 1536], P('night'), may hold values from -6 to 6
- inverse_var: float32 [8, 1536], P('night'), may hold values from 0.005 to 0.05
- prior: float32 [1536], replicated, may hold values from 0.5 to 5
Outputs:
- binned: bfloat16 [32, 16, 2, 1536], P('lst')
- weight_total: float32 [32, 16, 1536], P('lst')
Inputs may be any that keep to these rules, and one draw needn't show every extreme that they name: `offsets`: both -6 and 6 occur among the nights.
All inputs are finite; a program needn't handle non-finite values. No bound on the sum of `flags` on one device may be relied on, other than what follows from the above.
Results may differ from a plain program's by a relative error of at most 0.009.
Values may be sent and summed in bfloat16 or wider, within the bound.
A program may use at most 64 MiB of HBM per device.

v0:
```python
import jax
import jax.numpy as jnp
from jax import lax
from jax.sharding import PartitionSpec as P


def extended(x, sides, width):
    for axis, dim in sides:
        size, length = (lax.axis_size(axis), x.shape[dim])
        up = [(i, (i + 1) % size) for i in range(size)]
        down = [(j, i) for i, j in up]
        last = lax.slice_in_dim(x, length - width, length, axis=dim)
        first = lax.slice_in_dim(x, 0, width, axis=dim)
        before = lax.ppermute(last, axis, up)
        after = lax.ppermute(first, axis, down)
        x = jnp.concatenate([before, x, after], axis=dim)
    return x


def spline_taps(fraction):
    cube = fraction * fraction * fraction
    square = fraction * fraction
    first = (1.0 - fraction) ** 3 / 6.0
    second = (3.0 * cube - 6.0 * square + 4.0) / 6.0
    third = (-3.0 * cube + 3.0 * square + 3.0 * fraction + 1.0) / 6.0
    fourth = cube / 6.0
    return jnp.stack([first, second, third, fourth], axis=-1)


def shards(visibility, flags, counts, offsets, fraction, gains, inverse_var, prior):
    local_nights = visibility.shape[0]
    sample_count = visibility.shape[1]
    baseline_count = visibility.shape[2]
    channel_count = visibility.shape[4]
    scale = (flags * counts[:, :, None, None]).astype(jnp.float32) * inverse_var[:, None, None, :]
    weight = scale.astype(jnp.bfloat16)
    real_part = visibility[:, :, :, 0].astype(jnp.float32)
    imag_part = visibility[:, :, :, 1].astype(jnp.float32)
    gain_re = gains[:, 0][:, None, None, :]
    gain_im = gains[:, 1][:, None, None, :]
    cal_re = gain_re * real_part - gain_im * imag_part
    cal_im = gain_re * imag_part + gain_im * real_part
    weighted = (scale[:, :, :, None, :] * jnp.stack([cal_re, cal_im], axis=3)).astype(jnp.bfloat16)
    stacked = jnp.concatenate([weighted, weight[:, :, :, None, :]], axis=3)
    taps = spline_taps(fraction)
    tap_index = jnp.arange(4).reshape(1, 1, 1, 4)
    shifts = offsets.reshape(1, local_nights, 1, 1)
    tap_values = taps.reshape(1, local_nights, 1, 4)
    padded_slab = extended(stacked, (("lst", 1),), sample_count)
    out_row = jnp.arange(sample_count).reshape(sample_count, 1, 1, 1)
    source = jnp.arange(3 * sample_count).reshape(1, 1, 3 * sample_count, 1)
    target = out_row - shifts + tap_index - 1 + sample_count
    matrix = jnp.sum(jnp.where(source == target, tap_values, 0.0), axis=-1).astype(jnp.bfloat16)
    partial_numerator = jnp.dot(
        matrix.reshape(sample_count, local_nights * 3 * sample_count),
        padded_slab.reshape(local_nights * 3 * sample_count, baseline_count * 3 * channel_count),
        preferred_element_type=jnp.float32,
    )
    partial_numerator = partial_numerator.reshape(sample_count, baseline_count, 3, channel_count)
    totals = lax.psum(partial_numerator, "night")
    denominator_sum = totals[:, :, 2]
    binned = (
        totals[:, :, 0:2] / (denominator_sum[:, :, None, :] + prior[None, None, None, :])
    ).astype(jnp.bfloat16)
    return (binned, denominator_sum)


def solution(mesh):
    in_specs = (
        P("night", "lst", None, None, None),
        P("night", "lst", None, None),
        P("night", "lst"),
        P("night"),
        P("night"),
        P("night", None, None),
        P("night", None),
        P(),
    )
    out_specs = (P("lst", None, None, None), P("lst", None, None))
    return jax.shard_map(shards, mesh=mesh, in_specs=in_specs, out_specs=out_specs, check_vma=False)
```

profile of v0, /device:TPU:0, one launch (start us, length us, event | category | flops | bytes accessed | tf_op | source)
XLA Modules:
  0.0 172.8 jit_solution(5491326670959882846)
XLA Ops:
  7.2 0.0 copy-start.3
  7.2 0.0 copy-start.1
  7.2 0.0 copy-start.4
  7.2 0.0 all-reduce.2.cloned.1.call-start
  7.2 0.8 slice_reduce_fusion.1
  8.1 3.0 %fusion.11 = (bf16[1,8,16,1,1536]{4,3,2,1,0:T(2,128)(2,1)S(1)}, bf16[1,8,16,1,1536]{4,3,2,1,0:T(2,128)(2,1)S(1)}) fusion(bf16[1,8,16,2,1536]{4,3,2,1,0:T(2,128)(2,1)} %param.8), kind=kLoop, calls=%fused_computation.29 | loop fusion | bytes 1572864 | tf_op jit(solution)/shard_map/slice | solution.py:37
  11.1 0.0 copy-done.3
  11.2 0.0 copy-done.1
  11.2 0.0 copy-done.4
  11.2 0.2 fusion.7
  11.4 0.3 fusion.4
  11.7 0.1 fusion.3
  11.8 0.1 pad_maximum_fusion.1
  11.9 3.9 %collective-permute-start.1 = (bf16[1,8,16,3,1536]{4,2,3,1,0:T(8,128)(2,1)S(1)}, bf16[1,8,16,3,1536]{4,2,3,1,0:T(8,128)(2,1)S(1)}, u32[]{:S(2)}, u32[]{:S(2)}) collective-permute-start(bf16[1,8,16,3,1536]{4,2,3,1,0:T(8,128)(2,1)S(1)} %pad_maximum_fusion.1), channel_id=1, source_target_pairs={{8,0},{16,8},{24,16},{0,24},{9,1},{17,9},{25,17},{1,25},{10,2},{18... | collective-permute-start | bytes 3538952 | tf_op jit(solution)/shard_map/ppermute | solution.py:15
  15.9 0.0 collective-permute-start
  17.2 0.1 maximum_bitcast_fusion
  17.3 0.1 select_reduce_fusion
  17.4 24.9 %collective-permute-done.1 = bf16[1,8,16,3,1536]{4,2,3,1,0:T(8,128)(2,1)S(1)} collective-permute-done((bf16[1,8,16,3,1536]{4,2,3,1,0:T(8,128)(2,1)S(1)}, bf16[1,8,16,3,1536]{4,2,3,1,0:T(8,128)(2,1)S(1)}, u32[]{:S(2)}, u32[]{:S(2)}) %collective-permute-start.1) | collective-permute-done | bytes 1179680 | tf_op jit(solution)/shard_map/ppermute | solution.py:15
  42.3 25.1 %collective-permute-done = bf16[1,8,16,3,1536]{4,2,3,1,0:T(8,128)(2,1)S(1)} collective-permute-done((bf16[1,8,16,3,1536]{4,2,3,1,0:T(8,128)(2,1)S(1)}, bf16[1,8,16,3,1536]{4,2,3,1,0:T(8,128)(2,1)S(1)}, u32[]{:S(2)}, u32[]{:S(2)}) %collective-permute-start) | collective-permute-done | bytes 1179680 | tf_op jit(solution)/shard_map/ppermute | solution.py:14
  67.4 0.4 pad_maximum_fusion
  67.8 5.4 %copy.25 = bf16[1,24,16,3,1536]{4,3,2,1,0:T(4,128)(2,1)} copy(bf16[1,24,16,3,1536]{4,2,3,1,0:T(8,128)(2,1)S(1)} %pad_maximum_fusion) | data formatting | bytes 7077888 | tf_op jit(solution)/shard_map/concatenate | solution.py:16
  73.2 6.2 %reshape.136 = bf16[24,73728]{1,0:T(8,128)(2,1)S(1)} reshape(bf16[1,24,16,3,1536]{4,3,2,1,0:T(4,128)(2,1)} %copy.25) | data formatting | bytes 7077888 | tf_op jit(solution)/shard_map/reshape | solution.py:56
  79.4 6.2 %dot_general.8 = bf16[16,3,1536,24]{2,1,0,3:T(4,128)(2,1)} reshape(bf16[73728,24]{0,1:T(8,128)(2,1)S(1)} %bitcast.25) | data formatting | bytes 7077888 | tf_op jit(solution)/shard_map/dot_general | solution.py:54
  85.6 8.3 %fusion = f32[8,16,3,1536]{3,0,2,1:T(8,128)} fusion(bf16[16,3,1536,24]{2,1,0,3:T(4,128)(2,1)} %dot_general.8, bf16[8,24]{1,0:T(8,128)(2,1)S(1)} %select_reduce_fusion), kind=kOutput, calls=%fused_computation.1 | convolution fusion | flops 28311552 | bytes 5898624 | tf_op jit(solution)/shard_map/dot_general | solution.py:54
  93.8 0.0 all-reduce.2.cloned.1.call-update
  93.9 67.2 %all-reduce.2.cloned.1.call-done = f32[8,16,3,1536]{3,0,2,1:T(8,128)} async-done(((f32[8,16,3,1536]{3,0,2,1:T(8,128)}), f32[8,16,3,1536]{3,0,2,1:T(8,128)}) %all-reduce.2.cloned.1.call-update) | async-done | bytes 2359312 | tf_op jit(solution)/shard_map/psum | solution.py:60
  161.0 0.0 copy-done.2
  161.0 1.4 slice_bitcast_fusion
  162.5 0.4 copy-done
  162.9 0.2 fusion.2
  163.1 1.5 copy.27
  164.6 1.3 copy.28
  (5 shorter events, 0.0 us)
Async XLA Ops:
  7.2 4.0 %copy-start.3 = (f32[1,1536]{1,0:T(1,128)S(1)}, f32[1,1536]{1,0:T(1,128)}, u32[]{:S(2)}) copy-start(f32[1,1536]{1,0:T(1,128)} %param.14) | copy-start | bytes 18436
  7.2 4.0 %copy-start.1 = (s32[1,8,16,1536]{3,2,1,0:T(8,128)S(1)}, s32[1,8,16,1536]{3,2,1,0:T(8,128)}, u32[]{:S(2)}) copy-start(s32[1,8,16,1536]{3,2,1,0:T(8,128)} %param.9) | copy-start | bytes 2359300
  7.2 4.0 %copy-start.4 = (s32[1,8]{1,0:T(1,128)S(1)}, s32[1,8]{1,0:T(1,128)}, u32[]{:S(2)}) copy-start(s32[1,8]{1,0:T(1,128)} %param.10) | copy-start | bytes 100
  7.2 153.8 %all-reduce.2.cloned.1.call-start = ((), (), s32[]{:S(2)}) async-start(), calls=%async_computation | async-start | bytes 4718592 | tf_op jit(solution)/shard_map/psum | solution.py:60
  11.9 30.3 %collective-permute-start.1 = (bf16[1,8,16,3,1536]{4,2,3,1,0:T(8,128)(2,1)S(1)}, bf16[1,8,16,3,1536]{4,2,3,1,0:T(8,128)(2,1)S(1)}, u32[]{:S(2)}, u32[]{:S(2)}) collective-permute-start(bf16[1,8,16,3,1536]{4,2,3,1,0:T(8,128)(2,1)S(1)} %pad_maximum_fusion.1), channel_id=1, source_target_pairs={{8,0},{16,8},{24,16},{0,24},{9,1},{17,9},{25,17},{1,25},{10,2},{18... | collective-permute-start | bytes 3538952 | tf_op jit(solution)/shard_map/ppermute | solution.py:15
  15.9 51.5 %collective-permute-start = (bf16[1,8,16,3,1536]{4,2,3,1,0:T(8,128)(2,1)S(1)}, bf16[1,8,16,3,1536]{4,2,3,1,0:T(8,128)(2,1)S(1)}, u32[]{:S(2)}, u32[]{:S(2)}) collective-permute-start(bf16[1,8,16,3,1536]{4,2,3,1,0:T(8,128)(2,1)S(1)} %pad_maximum_fusion.1), channel_id=1, source_target_pairs={{0,8},{8,16},{16,24},{24,0},{1,9},{9,17},{17,25},{25,1},{2,10},{10... | collective-permute-start | bytes 3538952 | tf_op jit(solution)/shard_map/ppermute | solution.py:14
  93.8 67.2 %copy-start.2 = (f32[1536]{0:T(1024)S(1)}, f32[1536]{0:T(1024)}, u32[]{:S(2)}) copy-start(f32[1536]{0:T(1024)} %param.15) | copy-start | bytes 18436
  161.0 1.9 %copy-start = (f32[8,16,3,1536]{3,0,2,1:T(8,128)S(1)}, f32[8,16,3,1536]{3,0,2,1:T(8,128)}, u32[]{:S(2)}) copy-start(f32[8,16,3,1536]{3,0,2,1:T(8,128)} %all-reduce.2.cloned.1.call-done) | copy-start | bytes 7077892
Sparse Core Ops, SparseCore 0:
  94.0 67.0 all-reduce.1
where the time goes:
time: 173 us
  waiting for transfers between devices  117 us (68%)
  local copies, waits for them, and re-layouts  24.9 us (14%)
  between operations  15.5 us (9%)
  matrix products  8.26 us (5%)
  starting transfers between devices  3.99 us (2%)
  other arithmetic  2.95 us (2%)
    psum x1, waiting for transfers between devices, shards(): totals = lax.psum(partial_numerator, 'night')  67.2 us
    ppermute x1, waiting for transfers between devices, extended(): before = lax.ppermute(last, axis, up)  25.1 us
    ppermute x1, waiting for transfers between devices, extended(): after = lax.ppermute(first, axis, down)  24.9 us
    dot_general x1, matrix products, shards(): jnp.dot(matrix.reshape(sample_count, local_nights * 3 * sample_count), pa...  8.26 us
    dot_general x1, local copies, waits for them, and re-layouts, shards(): jnp.dot(matrix.reshape(sample_count, local_nights * 3 * sample_count), pa...  6.2 us
    reshape x1, local copies, waits for them, and re-layouts, shards(): padded_slab.reshape(local_nights * 3 * sample_count, baseline_count * 3 *...  6.2 us
    concatenate x1, local copies, waits for them, and re-layouts, extended(): x = jnp.concatenate([before, x, after], axis=dim)  5.36 us
    ppermute x1, starting transfers between devices, extended(): after = lax.ppermute(first, axis, down)  3.95 us
  transfers between devices with their start and end apart: 3, of which 3 were waited for; matrix products, arithmetic and copies ran while one was open for 0% of the time, Pallas kernels for 0%

commit v1 on v0

--- a/solution.py
+++ b/solution.py
@@ -2,6 +2,14 @@
 import jax.numpy as jnp
 from jax import lax
 from jax.sharding import PartitionSpec as P
+
+
+def doubling_sum(array, axis):
+    devices, total = (lax.axis_size(axis), array)
+    for far in [1 << k for k in range(devices.bit_length() - 1)]:
+        route = [(i, i ^ far) for i in range(devices)]
+        total = total + lax.ppermute(total, axis, route)
+    return total
 
 
 def extended(x, sides, width):
@@ -57,7 +65,7 @@
         preferred_element_type=jnp.float32,
     )
     partial_numerator = partial_numerator.reshape(sample_count, baseline_count, 3, channel_count)
-    totals = lax.psum(partial_numerator, "night")
+    totals = doubling_sum(partial_numerator, "night")
     denominator_sum = totals[:, :, 2]
     binned = (
         totals[:, :, 0:2] / (denominator_sum[:, :, None, :] + prior[None, None, None, :])

time: 173 us -> 252 us (1.46)
  waiting for transfers between devices: 117 us -> 208 us
  between operations: 15.5 us -> 2.13 us
  starting transfers between devices: 3.99 us -> 8.26 us
    ppermute x0 -> x3, waiting for transfers between devices: none -> 158 us  [doubling_sum(): total = total + lax.ppermute(total, axis, route)]
    psum x1 -> x0, waiting for transfers between devices: 67.2 us -> none  [shards(): totals = lax.psum(partial_numerator, 'night')]
    ppermute x0 -> x3, starting transfers between devices: none -> 4.32 us  [doubling_sum(): total = total + lax.ppermute(total, axis, route)]
  transfers between devices with their start and end apart: 3 -> 5, of which waited for: 3 -> 5; matrix products, arithmetic and copies ran while one was open for 0% -> 0% of each run, Pallas kernels for 0% -> 0%
where the time goes in v1:
time: 252 us
  waiting for transfers between devices  208 us (83%)
  local copies, waits for them, and re-layouts  24.5 us (10%)
  starting transfers between devices  8.26 us (3%)
  matrix products  6.82 us (3%)
  other arithmetic  2.83 us (1%)
    ppermute x3, waiting for transfers between devices, doubling_sum(): total = total + lax.ppermute(total, axis, route)  158 us
    ppermute x1, waiting for transfers between devices, extended(): before = lax.ppermute(last, axis, up)  25.1 us
    ppermute x1, waiting for transfers between devices, extended(): after = lax.ppermute(first, axis, down)  24.9 us
    dot_general x1, matrix products, shards(): jnp.dot(matrix.reshape(sample_count, local_nights * 3 * sample_count), pa...  6.82 us
    reshape x1, local copies, waits for them, and re-layouts, shards(): padded_slab.reshape(local_nights * 3 * sample_count, baseline_count * 3 *...  6.2 us
    dot_general x1, local copies, waits for them, and re-layouts, shards(): jnp.dot(matrix.reshape(sample_count, local_nights * 3 * sample_count), pa...  6.2 us
    concatenate x1, local copies, waits for them, and re-layouts, extended(): x = jnp.concatenate([before, x, after], axis=dim)  5.36 us
  transfers between devices with their start and end apart: 5, of which 5 were waited for; matrix products, arithmetic and copies ran while one was open for 0% of the time, Pallas kernels for 0%

profile of v1, /device:TPU:0, one launch (start us, length us, event | category | flops | bytes accessed | tf_op | source)
XLA Modules:
  0.0 252.1 jit_solution(7254685533747229039)
XLA Ops:
  0.6 0.0 copy-start.2
  0.7 0.8 slice_reduce_fusion.1
  1.5 3.0 %fusion.11 = (bf16[1,8,16,1,1536]{4,3,2,1,0:T(2,128)(2,1)S(1)}, bf16[1,8,16,1,1536]{4,3,2,1,0:T(2,128)(2,1)S(1)}) fusion(bf16[1,8,16,2,1536]{4,3,2,1,0:T(2,128)(2,1)} %param.8), kind=kLoop, calls=%fused_computation.29 | loop fusion | bytes 1572864 | tf_op jit(solution)/shard_map/slice | solution.py:45
  4.6 0.2 fusion.7
  4.8 0.3 fusion.4
  5.1 0.1 fusion.3
  5.2 0.1 pad_maximum_fusion.1
  5.3 3.9 %collective-permute-start.1 = (bf16[1,8,16,3,1536]{4,2,3,1,0:T(8,128)(2,1)S(1)}, bf16[1,8,16,3,1536]{4,2,3,1,0:T(8,128)(2,1)S(1)}, u32[]{:S(2)}, u32[]{:S(2)}) collective-permute-start(bf16[1,8,16,3,1536]{4,2,3,1,0:T(8,128)(2,1)S(1)} %pad_maximum_fusion.1), channel_id=1, source_target_pairs={{8,0},{16,8},{24,16},{0,24},{9,1},{17,9},{25,17},{1,25},{10,2},{18... | collective-permute-start | bytes 3538952 | tf_op jit(solution)/shard_map/ppermute | solution.py:23
  9.3 0.0 collective-permute-start
  10.6 0.1 maximum_bitcast_fusion
  10.7 0.1 select_reduce_fusion
  10.8 24.9 %collective-permute-done.1 = bf16[1,8,16,3,1536]{4,2,3,1,0:T(8,128)(2,1)S(1)} collective-permute-done((bf16[1,8,16,3,1536]{4,2,3,1,0:T(8,128)(2,1)S(1)}, bf16[1,8,16,3,1536]{4,2,3,1,0:T(8,128)(2,1)S(1)}, u32[]{:S(2)}, u32[]{:S(2)}) %collective-permute-start.1) | collective-permute-done | bytes 1179680 | tf_op jit(solution)/shard_map/ppermute | solution.py:23
  35.7 25.1 %collective-permute-done = bf16[1,8,16,3,1536]{4,2,3,1,0:T(8,128)(2,1)S(1)} collective-permute-done((bf16[1,8,16,3,1536]{4,2,3,1,0:T(8,128)(2,1)S(1)}, bf16[1,8,16,3,1536]{4,2,3,1,0:T(8,128)(2,1)S(1)}, u32[]{:S(2)}, u32[]{:S(2)}) %collective-permute-start) | collective-permute-done | bytes 1179680 | tf_op jit(solution)/shard_map/ppermute | solution.py:22
  60.8 0.4 pad_maximum_fusion
  61.2 5.4 %copy.25 = bf16[1,24,16,3,1536]{4,3,2,1,0:T(4,128)(2,1)} copy(bf16[1,24,16,3,1536]{4,2,3,1,0:T(8,128)(2,1)S(1)} %pad_maximum_fusion) | data formatting | bytes 7077888 | tf_op jit(solution)/shard_map/concatenate | solution.py:24
  66.6 6.2 %reshape.136 = bf16[24,73728]{1,0:T(8,128)(2,1)S(1)} reshape(bf16[1,24,16,3,1536]{4,3,2,1,0:T(4,128)(2,1)} %copy.25) | data formatting | bytes 7077888 | tf_op jit(solution)/shard_map/reshape | solution.py:64
  72.8 6.2 %dot_general.8 = bf16[16,3,1536,24]{2,1,0,3:T(4,128)(2,1)} reshape(bf16[73728,24]{0,1:T(8,128)(2,1)S(1)} %bitcast.25) | data formatting | bytes 7077888 | tf_op jit(solution)/shard_map/dot_general | solution.py:62
  79.0 6.8 %fusion = f32[8,16,3,1536]{3,0,2,1:T(8,128)S(1)} fusion(bf16[16,3,1536,24]{2,1,0,3:T(4,128)(2,1)} %dot_general.8, bf16[8,24]{1,0:T(8,128)(2,1)S(1)} %select_reduce_fusion), kind=kOutput, calls=%fused_computation.1 | convolution fusion | flops 28311552 | bytes 5898624 | tf_op jit(solution)/shard_map/dot_general | solution.py:62
  85.8 0.0 collective-permute-start.2
  85.8 4.5 %collective-permute-done.2 = f32[8,16,3,1536]{3,0,2,1:T(8,128)S(1)} collective-permute-done((f32[8,16,3,1536]{3,0,2,1:T(8,128)S(1)}, f32[8,16,3,1536]{3,0,2,1:T(8,128)S(1)}, u32[]{:S(2)}, u32[]{:S(2)}) %collective-permute-start.2) | collective-permute-done | bytes 2359328 | tf_op jit(solution)/shard_map/ppermute | solution.py:11
  90.3 0.4 add.79
  90.7 1.6 collective-permute-start.3
  92.4 51.7 %collective-permute-done.3 = f32[8,16,3,1536]{3,0,2,1:T(8,128)S(1)} collective-permute-done((f32[8,16,3,1536]{3,0,2,1:T(8,128)S(1)}, f32[8,16,3,1536]{3,0,2,1:T(8,128)S(1)}, u32[]{:S(2)}, u32[]{:S(2)}) %collective-permute-start.3) | collective-permute-done | bytes 2359328 | tf_op jit(solution)/shard_map/ppermute | solution.py:11
  144.1 0.4 add.80
  144.5 0.0 copy-start.1
  144.5 2.7 %collective-permute-start.4 = (f32[8,16,3,1536]{3,0,2,1:T(8,128)S(1)}, f32[8,16,3,1536]{3,0,2,1:T(8,128)S(1)}, u32[]{:S(2)}, u32[]{:S(2)}) collective-permute-start(f32[8,16,3,1536]{3,0,2,1:T(8,128)S(1)} %add.80), channel_id=1, source_target_pairs={{0,4},{1,5},{2,6},{3,7},{4,0},{5,1},{6,2},{7,3},{8,12},{9,13},{10,... | collective-permute-start | bytes 7077896 | tf_op jit(solution)/shard_map/ppermute | solution.py:11
  147.1 101.3 %collective-permute-done.4 = f32[8,16,3,1536]{3,0,2,1:T(8,128)S(1)} collective-permute-done((f32[8,16,3,1536]{3,0,2,1:T(8,128)S(1)}, f32[8,16,3,1536]{3,0,2,1:T(8,128)S(1)}, u32[]{:S(2)}, u32[]{:S(2)}) %collective-permute-start.4) | collective-permute-done | bytes 2359328 | tf_op jit(solution)/shard_map/ppermute | solution.py:11
  248.5 0.4 add.81
  248.8 0.2 slice_bitcast_fusion
  249.0 0.2 fusion.2
  249.2 1.5 copy.27
  250.7 1.3 copy.28
  (9 shorter events, 0.0 us)
Async XLA Ops:
  0.6 3.9 %copy-start.2 = (f32[1,1536]{1,0:T(1,128)S(1)}, f32[1,1536]{1,0:T(1,128)}, u32[]{:S(2)}) copy-start(f32[1,1536]{1,0:T(1,128)} %param.14) | copy-start | bytes 18436
  0.6 3.9 %copy-start = (s32[1,8,16,1536]{3,2,1,0:T(8,128)S(1)}, s32[1,8,16,1536]{3,2,1,0:T(8,128)}, u32[]{:S(2)}) copy-start(s32[1,8,16,1536]{3,2,1,0:T(8,128)} %param.9) | copy-start | bytes 2359300
  0.7 3.9 %copy-start.3 = (s32[1,8]{1,0:T(1,128)S(1)}, s32[1,8]{1,0:T(1,128)}, u32[]{:S(2)}) copy-start(s32[1,8]{1,0:T(1,128)} %param.10) | copy-start | bytes 100
  5.3 30.3 %collective-permute-start.1 = (bf16[1,8,16,3,1536]{4,2,3,1,0:T(8,128)(2,1)S(1)}, bf16[1,8,16,3,1536]{4,2,3,1,0:T(8,128)(2,1)S(1)}, u32[]{:S(2)}, u32[]{:S(2)}) collective-permute-start(bf16[1,8,16,3,1536]{4,2,3,1,0:T(8,128)(2,1)S(1)} %pad_maximum_fusion.1), channel_id=1, source_target_pairs={{8,0},{16,8},{24,16},{0,24},{9,1},{17,9},{25,17},{1,25},{10,2},{18... | collective-permute-start | bytes 3538952 | tf_op jit(solution)/shard_map/ppermute | solution.py:23
  9.3 51.5 %collective-permute-start = (bf16[1,8,16,3,1536]{4,2,3,1,0:T(8,128)(2,1)S(1)}, bf16[1,8,16,3,1536]{4,2,3,1,0:T(8,128)(2,1)S(1)}, u32[]{:S(2)}, u32[]{:S(2)}) collective-permute-start(bf16[1,8,16,3,1536]{4,2,3,1,0:T(8,128)(2,1)S(1)} %pad_maximum_fusion.1), channel_id=1, source_target_pairs={{0,8},{8,16},{16,24},{24,0},{1,9},{9,17},{17,25},{25,1},{2,10},{10... | collective-permute-start | bytes 3538952 | tf_op jit(solution)/shard_map/ppermute | solution.py:22
  85.8 4.5 %collective-permute-start.2 = (f32[8,16,3,1536]{3,0,2,1:T(8,128)S(1)}, f32[8,16,3,1536]{3,0,2,1:T(8,128)S(1)}, u32[]{:S(2)}, u32[]{:S(2)}) collective-permute-start(f32[8,16,3,1536]{3,0,2,1:T(8,128)S(1)} %fusion), channel_id=1, source_target_pairs={{0,1},{1,0},{2,3},{3,2},{4,5},{5,4},{6,7},{7,6},{8,9},{9,8},{10,11... | collective-permute-start | bytes 7077896 | tf_op jit(solution)/shard_map/ppermute | solution.py:11
  90.7 53.4 %collective-permute-start.3 = (f32[8,16,3,1536]{3,0,2,1:T(8,128)S(1)}, f32[8,16,3,1536]{3,0,2,1:T(8,128)S(1)}, u32[]{:S(2)}, u32[]{:S(2)}) collective-permute-start(f32[8,16,3,1536]{3,0,2,1:T(8,128)S(1)} %add.79), channel_id=1, source_target_pairs={{0,2},{1,3},{2,0},{3,1},{4,6},{5,7},{6,4},{7,5},{8,10},{9,11},{10,... | collective-permute-start | bytes 7077896 | tf_op jit(solution)/shard_map/ppermute | solution.py:11
  144.5 104.4 %copy-start.1 = (f32[1536]{0:T(1024)S(1)}, f32[1536]{0:T(1024)}, u32[]{:S(2)}) copy-start(f32[1536]{0:T(1024)} %param.15) | copy-start | bytes 18436
  144.5 104.0 %collective-permute-start.4 = (f32[8,16,3,1536]{3,0,2,1:T(8,128)S(1)}, f32[8,16,3,1536]{3,0,2,1:T(8,128)S(1)}, u32[]{:S(2)}, u32[]{:S(2)}) collective-permute-start(f32[8,16,3,1536]{3,0,2,1:T(8,128)S(1)} %add.80), channel_id=1, source_target_pairs={{0,4},{1,5},{2,6},{3,7},{4,0},{5,1},{6,2},{7,3},{8,12},{9,13},{10,... | collective-permute-start | bytes 7077896 | tf_op jit(solution)/shard_map/ppermute | solution.py:11
